TPU v7x, 512 devices: a whole 4x8x8 slice. The times are simulated.
512 devices in a mesh: blk: 32 (over y, x), lev: 16 (over z, core).
Axes of the slice: x: 4, y: 8, z: 8, core: 2. Of those that a mesh axis runs over, the one named last changes fastest.
Arguments:
- grid_values: float32 [64, 2, 64, 6144], P('blk', None, 'lev'), may hold values from -6 to 6
- quad_weight: float32 [64], P('blk'), may hold values from 0.3 to 3
- legendre: bfloat16 [1024, 2, 64, 512], P('blk'), may hold values from -0.75 to 0.75
- vertical_modes: float32 [64, 64], replicated, may hold values from -0.75 to 0.75
- eigenvalues: float32 [64], replicated, may hold values from 0.05 to 5
- pair_latitude: int32 [64], P('blk'), may hold values from 0 to 1279, as said below
- wave_slot: int32 [1024], replicated, may hold values from 0 to 1023, each once
Outputs:
- new_grid: float32 [64, 2, 64, 6144], P('blk', None, 'lev')
Inputs may be any that keep to these rules, and one draw needn't show every extreme that they name: `pair_latitude`: distinct northern cycle indices; cycle r has 20 + 4 r points and so has its southern mirror; cycles 0 and 1279 are always among them. `wave_slot`: each wavenumber is held at exactly one position.
All inputs are finite; a program needn't handle non-finite values.
Results may differ from a plain program's by a relative error of at most 0.0043.
Values may be sent and summed in bfloat16 or wider, within the bound.
A program may use at most 64 MiB of HBM per device.

v0:
```python
import jax
import jax.numpy as jnp
from jax import lax
from jax.experimental import pallas as pl
from jax.experimental.pallas import tpu as pltpu
from jax.sharding import PartitionSpec as P

MESH = pl.DeviceIdType.MESH
BF16 = jnp.bfloat16
F32 = jnp.float32

WAVES = 1024
HALF = 512
LEVELS = 64
NB = 32
NL = 16
SPAN = 256
BLOCKS = 22
ROWS = 8 * BLOCKS
TILES = WAVES // 128
LIVE = BLOCKS * SPAN
PSLOT = 6144
IMPLICIT_FACTOR = 4.0
PI = 3.141592653589793


def iota(shape, dim):
    return lax.broadcasted_iota(jnp.int32, shape, dim)


def dot(a, b):
    return jnp.dot(a, b, preferred_element_type=F32)


def dot_nt(a, b):
    return lax.dot_general(a, b, (((1,), (1,)), ((), ())), preferred_element_type=F32)


def dot_tn(a, b):
    return lax.dot_general(a, b, (((0,), (0,)), ((), ())), preferred_element_type=F32)


def split(x):
    high = x.astype(BF16)
    return high, (x - high.astype(F32)).astype(BF16)


def rotation(phase, points, inverse):
    turns = jnp.floor(phase * inverse + 0.5)
    x = (phase - turns * points) * inverse
    z = x * x
    sine = 0.0
    cosine = 0.0
    sin_terms = [PI]
    cos_terms = [1.0]
    for k in range(1, 7):
        sin_terms.append(-sin_terms[-1] * PI * PI / ((2 * k) * (2 * k + 1)))
        cos_terms.append(-cos_terms[-1] * PI * PI / ((2 * k - 1) * (2 * k)))
    sine = jnp.full_like(z, sin_terms[6])
    cosine = jnp.full_like(z, cos_terms[6])
    for k in range(5, -1, -1):
        sine = sine * z + sin_terms[k]
        cosine = cosine * z + cos_terms[k]
    sine = sine * x
    return 1.0 - 2.0 * sine * sine, -2.0 * sine * cosine


def turn(a, b):
    return a[0] * b[0] - a[1] * b[1], a[0] * b[1] + a[1] * b[0]


def stack(parts):
    return jnp.concatenate(parts, axis=0)


def kernel(
    grid_hbm, weight_ref, legendre_hbm, modes_ref, rates_ref, cycle_ref, slot_ref, slot_smem,
    out_ref,
    grid_ref, raw_ref, wave_ref, x_ref, table_ref, turn_ref, four_ref,
    s1_ref, r1_ref, s2_ref, r2_ref, s3_ref, r3_ref, s4_ref, r4_ref,
    leg_ref, mode1_ref, mode2_ref, damp_ref, solved_ref, turned_ref,
    load_sem, send_sem, recv_sem,
):
    blk = lax.axis_index("blk")
    lev = lax.axis_index("lev")

    barrier = pltpu.get_barrier_semaphore()

    def greet_blk(k, carry):
        pl.semaphore_signal(barrier, inc=1, device_id=((blk + k) % NB, lev), device_id_type=MESH)
        return carry

    def greet_lev(k, carry):
        pl.semaphore_signal(barrier, inc=1, device_id=(blk, (lev + k) % NL), device_id_type=MESH)
        return carry

    grid_copy = pltpu.make_async_copy(grid_hbm, grid_ref, load_sem.at[0])
    grid_copy.start()
    legendre_copy = pltpu.make_async_copy(
        legendre_hbm.at[pl.ds(2 * lev, 2)], raw_ref, load_sem.at[1]
    )
    legendre_copy.start()
    lax.fori_loop(1, NB, greet_blk, 0)
    lax.fori_loop(1, NL, greet_lev, 0)

    column = iota((128, WAVES), 1)
    pick = (iota((128, WAVES), 0) == 32 * (column & 3) + (column >> 5)).astype(F32).astype(BF16)
    slots = slot_ref[...]
    halves = stack([slots >> 5, slots & 31]).astype(F32).astype(BF16)
    spread = dot(halves, pick)
    column = iota((8, WAVES), 1)
    mine = iota((8, WAVES), 0) == ((column & 31) >> 2)
    spread = jnp.where(mine, 32.0 * spread[:8] + spread[8:], 0.0)
    waves = jnp.sum(spread, axis=0, keepdims=True)
    for tile in range(TILES):
        wave_ref[tile] = jnp.broadcast_to(waves[:, 128 * tile : 128 * (tile + 1)], (8, 128))

    def points_of(i):
        return 20 + 4 * cycle_ref[i]

    grid_copy.wait()

    def fold_step(step, carry):
        i = step // (BLOCKS // 2)
        k = step % (BLOCKS // 2)
        points = points_of(i)
        scale = jnp.full((4, SPAN), weight_ref[i], F32) / jnp.full((4, SPAN), points, jnp.int32).astype(F32)
        rows = []
        for half in range(2):
            start = pl.multiple_of(512 * k + 256 * half, 256)
            live = iota((4, SPAN), 1) + start < points
            north = grid_ref[i, 0, :, pl.ds(start, SPAN)]
            south = grid_ref[i, 1, :, pl.ds(start, SPAN)]
            rows.append(jnp.where(live, (north + south) * scale, 0.0))
            rows.append(jnp.where(live, (north - south) * scale, 0.0))
        high, low = split(stack(rows))
        x_ref[i, 0, pl.ds(pl.multiple_of(16 * k, 16), 16), :] = high
        x_ref[i, 1, pl.ds(pl.multiple_of(16 * k, 16), 16), :] = low
        return carry

    lax.fori_loop(0, BLOCKS, fold_step, 0)

    def analyse_step(step, carry):
        i = step // TILES
        tile = step % TILES
        points = jnp.full((8, 128), points_of(i), jnp.int32).astype(F32)
        inverse = 1.0 / points
        wave = wave_ref[tile]
        row = iota((8, 128), 0)
        place = row.astype(F32)
        extra = jnp.where(row == 0, 8.0, jnp.where(row == 1, 128.0, 2048.0))
        fine = rotation(place * wave, points, inverse)
        coarse = rotation(16.0 * place * wave, points, inverse)
        block = rotation(256.0 * place * wave, points, inverse)
        jump = rotation(extra * wave, points, inverse)

        def spread_row(pair, k, rows=8):
            return tuple(jnp.broadcast_to(part[k : k + 1], (rows, 128)) for part in pair)

        fine_next = turn(fine, spread_row(jump, 0))
        coarse_next = turn(coarse, spread_row(jump, 1))
        leap = spread_row(jump, 2)
        kept = (2.0 * wave < points).astype(F32)
        block = (block[0] * kept, block[1] * kept)
        block_1 = turn(block, leap)
        block_2 = turn(block_1, leap)

        high = [[], []]
        low = [[], []]
        for a in range(16):
            lead = spread_row(coarse if a < 8 else coarse_next, a % 8)
            first = turn(lead, fine)
            second = turn(lead, fine_next)
            for part in range(2):
                h, l = split(stack([first[part], second[part]]))
                high[part].append(h)
                low[part].append(l)
        for part in range(2):
            table_ref[i, tile, :, 128 * part : 128 * (part + 1)] = stack(high[part])
        fine_table = table_ref[i, tile]
        rest_table = jnp.concatenate([stack(low[0]), stack(low[1])], axis=1)
        x_high = x_ref[i, 0]
        sums = dot(x_high, fine_table) + dot(x_ref[i, 1], fine_table) + dot(x_high, rest_table)
        real = jnp.zeros((8, 128), F32)
        imag = jnp.zeros((8, 128), F32)
        for u in range(BLOCKS):
            c, s = spread_row((block, block_1, block_2)[u // 8], u % 8)
            turn_ref[i, tile, 0, u] = c
            turn_ref[i, tile, 1, u] = s
            p, q = sums[8 * u : 8 * u + 8, :128], sums[8 * u : 8 * u + 8, 128:]
            real = real + (c * p - s * q)
            imag = imag + (c * q + s * p)
        start = pl.multiple_of(16 * tile, 16)
        four_ref[i, pl.ds(start, 8), :] = real
        four_ref[i, pl.ds(start + 8, 8), :] = imag
        return carry

    lax.fori_loop(0, 2 * TILES, analyse_step, 0)

    for i in range(2):
        flipped = four_ref[i].T
        for a in range(4):
            s1_ref[pl.ds(2 * a + i, NB, stride=8), :] = flipped[NB * a : NB * (a + 1)]
    own = pl.ds(pl.multiple_of(8 * blk, 8), 8)
    r1_ref[own, :] = s1_ref[own, :]
    pl.semaphore_wait(barrier, NB + NL - 2)

    def send_blk(source, target, sem):
        def step(k, carry):
            other = (blk + k) % NB
            pltpu.make_async_remote_copy(
                src_ref=source.at[pl.ds(pl.multiple_of(8 * other, 8), 8)],
                dst_ref=target.at[own],
                send_sem=send_sem.at[sem],
                recv_sem=recv_sem.at[sem],
                device_id=(other, lev),
                device_id_type=MESH,
            ).start()
            return carry

        lax.fori_loop(1, NB, step, 0)
        rows = pl.ds(0, 8 * (NB - 1))
        return pltpu.make_async_remote_copy(
            src_ref=source.at[rows], dst_ref=target.at[rows],
            send_sem=send_sem.at[sem], recv_sem=recv_sem.at[sem],
            device_id=((blk + 1) % NB, lev), device_id_type=MESH,
        )

    def send_lev(source, target, sem):
        def step(k, carry):
            other = (lev + k) % NL
            pltpu.make_async_remote_copy(
                src_ref=source.at[other],
                dst_ref=target.at[lev],
                send_sem=send_sem.at[sem],
                recv_sem=recv_sem.at[sem],
                device_id=(blk, other),
                device_id_type=MESH,
            ).start()
            return carry

        lax.fori_loop(1, NL, step, 0)
        rows = pl.ds(0, NL - 1)
        return pltpu.make_async_remote_copy(
            src_ref=source.at[rows], dst_ref=target.at[rows],
            send_sem=send_sem.at[sem], recv_sem=recv_sem.at[sem],
            device_id=(blk, (lev + 1) % NL), device_id_type=MESH,
        )

    sent_1 = send_blk(s1_ref, r1_ref, 0)

    legendre_copy.wait()
    wave_0 = slot_smem[32 * blk + 2 * lev]
    wave_1 = slot_smem[32 * blk + 2 * lev + 1]
    row = iota((256, 256), 0)
    source = ((row >> 6) & 1) * 128 + (row >> 7) * 64 + 2 * (row & 31) + ((row >> 5) & 1)
    reorder = (iota((256, 256), 1) == source).astype(F32).astype(BF16)
    ordered = dot(reorder, raw_ref[...].reshape(256, HALF))
    row = iota((256, HALF), 0)
    degree = jnp.where(((row >> 6) & 1) == 0, wave_0, wave_1) + (row >> 7) + 2 * iota((256, HALF), 1)
    leg_ref[...] = jnp.where(degree <= WAVES - 1, ordered, 0.0).astype(BF16)

    def spread_rows(shape, row_dim):
        row = iota(shape, row_dim)
        return iota(shape, 1 - row_dim) == 4 * (row >> 4) + (row & 3)

    tall = spread_rows((256, LEVELS), 0).astype(F32).astype(BF16)
    wide = spread_rows((LEVELS, 256), 1).astype(F32).astype(BF16)
    same = ((iota((256, 256), 0) >> 2) & 3) == ((iota((256, 256), 1) >> 2) & 3)
    for part, modes in enumerate(split(modes_ref[...])):
        full = dot(tall, dot(modes, wide).astype(BF16))
        mode2_ref[256 * part : 256 * (part + 1), :] = jnp.where(same, full, 0.0).astype(BF16)
        full = dot(tall, dot_tn(modes, wide).astype(BF16))
        mode1_ref[256 * part : 256 * (part + 1), :] = jnp.where(same, full, 0.0).astype(BF16)

    rate = jnp.sum(
        jnp.where(spread_rows((256, LEVELS), 0), jnp.broadcast_to(rates_ref[...], (256, LEVELS)), 0.0),
        axis=1, keepdims=True,
    )
    rate = jnp.broadcast_to(rate, (256, 128))

    def damp_step(step, carry):
        e = step // 4
        chunk = step % 4
        wave = jnp.where(e == 0, wave_0, wave_1)
        degree = wave + ((iota((256, 128), 0) >> 2) & 1) + 2 * (iota((256, 128), 1) + 128 * chunk)
        degree = degree.astype(F32)
        term = degree * (degree + 1.0) * (IMPLICIT_FACTOR / (WAVES * (WAVES - 1)))
        stiffness = term * rate
        damp_ref[e, chunk] = stiffness / (1.0 + stiffness)
        return carry

    lax.fori_loop(0, 8, damp_step, 0)

    sent_1.wait_recv()

    for a in range(2):
        block = stack([r1_ref[pl.ds(4 * a + j, NB, stride=8), :] for j in range(4)]).T.astype(BF16)
        for t in range(8):
            s2_ref[2 * t + a] = block[16 * t : 16 * (t + 1)]
    r2_ref[lev] = s2_ref[lev]
    sent_2 = send_lev(s2_ref, r2_ref, 1)
    sent_2.wait_recv()

    data = r2_ref[...].reshape(256, 128)
    parity = (iota((256, 128), 0) >> 2) & 1
    side = iota((256, 128), 1) >> 6

    def chosen(q, e):
        return ((parity == q) & (side == e)).astype(F32).astype(BF16)

    def solve_step(step, carry):
        for e in range(2):
            columns = pl.ds(pl.multiple_of(256 * step, 256), 256)
            left = jnp.concatenate([data * chosen(0, e), data * chosen(1, e)], axis=1)
            spectral = dot(left, leg_ref[:, columns])
            high, low = split(spectral)
            both = dot(mode1_ref[...], high)
            modal = both[:256] + both[256:] + dot(mode1_ref[:256], low)
            damping = jnp.concatenate([damp_ref[e, 2 * step], damp_ref[e, 2 * step + 1]], axis=1)
            high, low = split(modal * damping)
            both = dot(mode2_ref[...], high)
            change = both[:256] + both[256:] + dot(mode2_ref[:256], low)
            solved_ref[e, :, columns] = (spectral - change).astype(BF16)
        return carry

    lax.fori_loop(0, 2, solve_step, 0)

    picked = []
    for e in range(2):
        back = dot_nt(solved_ref[e], leg_ref[...])
        picked.append(jnp.where(parity == 0, back[:, :128], back[:, 128:]))
    s3_ref[...] = jnp.where(side == 0, picked[0], picked[1]).astype(BF16).reshape(NL, 16, 128)
    r3_ref[lev] = s3_ref[lev]
    sent_3 = send_lev(s3_ref, r3_ref, 2)
    sent_3.wait_recv()

    for a in range(2):
        block = stack([r3_ref[2 * t + a] for t in range(8)]).astype(F32).T
        for j in range(4):
            s4_ref[pl.ds(4 * a + j, NB, stride=8), :] = block[NB * j : NB * (j + 1)]
    r4_ref[own, :] = s4_ref[own, :]
    sent_4 = send_blk(s4_ref, r4_ref, 3)
    out_ref[:, :, :, pl.ds(LIVE, PSLOT - LIVE)] = jnp.zeros((2, 2, 4, PSLOT - LIVE), F32)
    sent_4.wait_recv()

    for i in range(2):
        four_ref[i] = stack([r4_ref[pl.ds(2 * a + i, NB, stride=8), :] for a in range(4)]).T

    def turn_step(step, carry):
        i = step // TILES
        tile = step % TILES
        wave = wave_ref[tile]
        double = jnp.where(wave == 0.0, 1.0, 2.0)
        start = pl.multiple_of(16 * tile, 16)
        real = four_ref[i, pl.ds(start, 8), :] * double
        imag = four_ref[i, pl.ds(start + 8, 8), :] * double
        for k in range(BLOCKS // 2):
            reals, imags = [], []
            for u in (2 * k, 2 * k + 1):
                c = turn_ref[i, tile, 0, u]
                s = turn_ref[i, tile, 1, u]
                reals.append(real * c + imag * s)
                imags.append(imag * c - real * s)
            for part, rows in enumerate((reals, imags)):
                high, low = split(stack(rows))
                lanes = slice(128 * part, 128 * (part + 1))
                turned_ref[i, tile, 16 * k : 16 * k + 16, lanes] = high
                turned_ref[i, tile, ROWS + 16 * k : ROWS + 16 * k + 16, lanes] = low
        return carry

    lax.fori_loop(0, 2 * TILES, turn_step, 0)

    for i in range(2):
        left = jnp.concatenate([turned_ref[i, tile] for tile in range(TILES)], axis=1)
        right = jnp.concatenate([table_ref[i, tile] for tile in range(TILES)], axis=1)
        both = dot_nt(left, right)
        points = points_of(i)
        for u in range(BLOCKS):
            value = both[8 * u : 8 * u + 8] + both[ROWS + 8 * u : ROWS + 8 * u + 8]
            live = iota((4, SPAN), 1) + SPAN * u < points
            out_ref[i, 0, :, SPAN * u : SPAN * (u + 1)] = jnp.where(live, value[:4] + value[4:], 0.0)
            out_ref[i, 1, :, SPAN * u : SPAN * (u + 1)] = jnp.where(live, value[:4] - value[4:], 0.0)

    for sent in (sent_1, sent_2, sent_3, sent_4):
        sent.wait_send()


def shards(grid_values, quad_weight, legendre, vertical_modes, eigenvalues, pair_latitude, wave_slot):
    vmem = pl.BlockSpec(memory_space=pltpu.VMEM)
    smem = pl.BlockSpec(memory_space=pltpu.SMEM)
    hbm = pl.BlockSpec(memory_space=pl.ANY)
    return pl.pallas_call(
        kernel,
        out_shape=jax.ShapeDtypeStruct(grid_values.shape, F32),
        in_specs=[hbm, smem, hbm, vmem, vmem, smem, vmem, smem],
        out_specs=vmem,
        scratch_shapes=[
            pltpu.VMEM((2, 2, 4, PSLOT), F32),
            pltpu.VMEM((2, 2, 64, HALF), BF16),
            pltpu.VMEM((TILES, 8, 128), F32),
            pltpu.VMEM((2, 2, ROWS, SPAN), BF16),
            pltpu.VMEM((2, TILES, SPAN, 256), BF16),
            pltpu.VMEM((2, TILES, 2, BLOCKS, 8, 128), F32),
            pltpu.VMEM((2, 128, 128), F32),
            pltpu.VMEM((8 * NB, 128), F32),
            pltpu.VMEM((8 * NB, 128), F32),
            pltpu.VMEM((NL, 16, 128), BF16),
            pltpu.VMEM((NL, 16, 128), BF16),
            pltpu.VMEM((NL, 16, 128), BF16),
            pltpu.VMEM((NL, 16, 128), BF16),
            pltpu.VMEM((8 * NB, 128), F32),
            pltpu.VMEM((8 * NB, 128), F32),
            pltpu.VMEM((256, HALF), BF16),
            pltpu.VMEM((512, 256), BF16),
            pltpu.VMEM((512, 256), BF16),
            pltpu.VMEM((2, 4, 256, 128), F32),
            pltpu.VMEM((2, 256, HALF), BF16),
            pltpu.VMEM((2, TILES, 2 * ROWS, 256), BF16),
            pltpu.SemaphoreType.DMA((2,)),
            pltpu.SemaphoreType.DMA((4,)),
            pltpu.SemaphoreType.DMA((4,)),
        ],
        compiler_params=pltpu.CompilerParams(
            collective_id=0, has_side_effects=True, vmem_limit_bytes=62 * 1024 * 1024
        ),
        cost_estimate=pl.CostEstimate(flops=4_000_000_000, bytes_accessed=1_500_000, transcendentals=0),
    )(
        grid_values, quad_weight, legendre, vertical_modes, eigenvalues.reshape(1, LEVELS),
        pair_latitude, wave_slot.reshape(8, 128), wave_slot,
    )


def solution(mesh):
    in_specs = (
        P("blk", None, "lev", None),
        P("blk"),
        P("blk", None, None, None),
        P(),
        P(),
        P("blk"),
        P(),
    )
    out_specs = P("blk", None, "lev", None)
    return jax.shard_map(shards, mesh=mesh, in_specs=in_specs, out_specs=out_specs, check_vma=False)
```

profile of v0, /device:TPU:1, one launch (start us, length us, event | category | flops | bytes accessed | tf_op | source)
XLA Modules:
  0.0 48.6 jit_solution(6847859122529724413)
XLA Ops:
  0.0 46.9 %shard_map.73 = f32[2,2,4,6144]{3,2,1,0:T(4,128)} custom-call(f32[2,2,4,6144]{3,2,1,0:T(4,128)} %grid_hbm.1, f32[2]{0:T(128)} %weight_ref.1, bf16[32,2,64,512]{3,2,1,0:T(8,128)(2,1)} %legendre_hbm.1, f32[64,64]{1,0:T(8,128)} %modes_ref.1, f32[1,64]{1,0:T(1,128)} %bitcast.3, s32[2]{0:T(128)} %cycle_ref.1, s32[8,128]{1,0:T(8,128)} %bitcast.2, s32[1024]{0:T(1024)} %slot_smem.1), custom_call_target="tpu_custom_call" | custom-call | flops 4000000000 | bytes 1500000 | tf_op jit(solution)/shard_map/pallas_call | solution.py:393
  46.9 1.8 %copy.9 = f32[2,2,4,6144]{3,2,1,0:T(4,128)} copy(f32[2,2,4,6144]{3,2,1,0:T(4,128)} %shard_map.73) | data formatting | bytes 786432
where the time goes:
time: 48.9 us; the launch traced here: 48.6 us
  Pallas kernels  46.9 us (96%)
  local copies, waits for them, and re-layouts  1.77 us (4%)
    pallas_call x1, Pallas kernels, shards(): pl.pallas_call(kernel, out_shape=jax.ShapeDtypeStruct(grid_values.shape,...  46.9 us
    unnamed x1, local copies, waits for them, and re-layouts  1.77 us

commit v1 on v0

--- a/solution.py
+++ b/solution.py
@@ -22,6 +22,28 @@
 PSLOT = 6144
 IMPLICIT_FACTOR = 4.0
 PI = 3.141592653589793
+
+
+def ring(step, size):
+    return min(step, size - step)
+
+
+BLK_PEERS = sorted(
+    [(y, x) for y in range(8) for x in range(4) if (y, x) != (0, 0)],
+    key=lambda d: (-ring(d[0], 8) - ring(d[1], 4), d),
+)
+LEV_PEERS = sorted(
+    [(z, c) for z in range(8) for c in range(2) if (z, c) != (0, 0)],
+    key=lambda d: (-ring(d[0], 8) - 0.5 * d[1], d),
+)
+
+
+def blk_peer(blk, peer):
+    return (blk // 4 + peer[0]) % 8 * 4 + (blk % 4 + peer[1]) % 4
+
+
+def lev_peer(lev, peer):
+    return (lev // 2 + peer[0]) % 8 * 2 + (lev % 2 + peer[1]) % 2
 
 
 def iota(shape, dim):
@@ -77,7 +99,7 @@
     grid_hbm, weight_ref, legendre_hbm, modes_ref, rates_ref, cycle_ref, slot_ref, slot_smem,
     out_ref,
     grid_ref, raw_ref, wave_ref, x_ref, table_ref, turn_ref, four_ref,
-    s1_ref, r1_ref, s2_ref, r2_ref, s3_ref, r3_ref, s4_ref, r4_ref,
+    rows_ref, s1_ref, r1_ref, s2_ref, r2_ref, s3_ref, r3_ref, s4_ref, r4_ref,
     leg_ref, mode1_ref, mode2_ref, damp_ref, solved_ref, turned_ref,
     load_sem, send_sem, recv_sem,
 ):
@@ -85,14 +107,6 @@
     lev = lax.axis_index("lev")
 
     barrier = pltpu.get_barrier_semaphore()
-
-    def greet_blk(k, carry):
-        pl.semaphore_signal(barrier, inc=1, device_id=((blk + k) % NB, lev), device_id_type=MESH)
-        return carry
-
-    def greet_lev(k, carry):
-        pl.semaphore_signal(barrier, inc=1, device_id=(blk, (lev + k) % NL), device_id_type=MESH)
-        return carry
 
     grid_copy = pltpu.make_async_copy(grid_hbm, grid_ref, load_sem.at[0])
     grid_copy.start()
@@ -100,8 +114,10 @@
         legendre_hbm.at[pl.ds(2 * lev, 2)], raw_ref, load_sem.at[1]
     )
     legendre_copy.start()
-    lax.fori_loop(1, NB, greet_blk, 0)
-    lax.fori_loop(1, NL, greet_lev, 0)
+    for peer in BLK_PEERS:
+        pl.semaphore_signal(barrier, inc=1, device_id=(blk_peer(blk, peer), lev), device_id_type=MESH)
+    for peer in LEV_PEERS:
+        pl.semaphore_signal(barrier, inc=1, device_id=(blk, lev_peer(lev, peer)), device_id_type=MESH)
 
     column = iota((128, WAVES), 1)
     pick = (iota((128, WAVES), 0) == 32 * (column & 3) + (column >> 5)).astype(F32).astype(BF16)
@@ -175,12 +191,14 @@
                 h, l = split(stack([first[part], second[part]]))
                 high[part].append(h)
                 low[part].append(l)
-        for part in range(2):
-            table_ref[i, tile, :, 128 * part : 128 * (part + 1)] = stack(high[part])
-        fine_table = table_ref[i, tile]
-        rest_table = jnp.concatenate([stack(low[0]), stack(low[1])], axis=1)
+        table = jnp.concatenate([stack(high[0]), stack(high[1])], axis=1)
+        rest = jnp.concatenate([stack(low[0]), stack(low[1])], axis=1)
+        table_ref[i, :, pl.ds(pl.multiple_of(256 * tile, 256), 256)] = table
         x_high = x_ref[i, 0]
-        sums = dot(x_high, fine_table) + dot(x_ref[i, 1], fine_table) + dot(x_high, rest_table)
+        sums = dot(
+            jnp.concatenate([x_high, x_ref[i, 1], x_high], axis=1),
+            jnp.concatenate([table, table, rest], axis=0),
+        )
         real = jnp.zeros((8, 128), F32)
         imag = jnp.zeros((8, 128), F32)
         for u in range(BLOCKS):
@@ -195,40 +213,37 @@
         four_ref[i, pl.ds(start + 8, 8), :] = imag
         return carry
 
-    lax.fori_loop(0, 2 * TILES, analyse_step, 0)
+    lax.fori_loop(0, 2 * TILES, analyse_step, 0, unroll=4)
 
     for i in range(2):
         flipped = four_ref[i].T
         for a in range(4):
-            s1_ref[pl.ds(2 * a + i, NB, stride=8), :] = flipped[NB * a : NB * (a + 1)]
-    own = pl.ds(pl.multiple_of(8 * blk, 8), 8)
-    r1_ref[own, :] = s1_ref[own, :]
+            rows_ref[pl.ds(2 * a + i, NB, stride=8), :] = flipped[NB * a : NB * (a + 1)]
+    s1_ref[...] = rows_ref[...].astype(BF16).reshape(NB, 8, 128)
+    r1_ref[blk] = s1_ref[blk]
     pl.semaphore_wait(barrier, NB + NL - 2)
 
     def send_blk(source, target, sem):
-        def step(k, carry):
-            other = (blk + k) % NB
+        for peer in BLK_PEERS:
+            other = blk_peer(blk, peer)
             pltpu.make_async_remote_copy(
-                src_ref=source.at[pl.ds(pl.multiple_of(8 * other, 8), 8)],
-                dst_ref=target.at[own],
+                src_ref=source.at[other],
+                dst_ref=target.at[blk],
                 send_sem=send_sem.at[sem],
                 recv_sem=recv_sem.at[sem],
                 device_id=(other, lev),
                 device_id_type=MESH,
             ).start()
-            return carry
-
-        lax.fori_loop(1, NB, step, 0)
-        rows = pl.ds(0, 8 * (NB - 1))
+        rows = pl.ds(0, NB - 1)
         return pltpu.make_async_remote_copy(
             src_ref=source.at[rows], dst_ref=target.at[rows],
             send_sem=send_sem.at[sem], recv_sem=recv_sem.at[sem],
-            device_id=((blk + 1) % NB, lev), device_id_type=MESH,
+            device_id=(blk_peer(blk, BLK_PEERS[0]), lev), device_id_type=MESH,
         )
 
     def send_lev(source, target, sem):
-        def step(k, carry):
-            other = (lev + k) % NL
+        for peer in LEV_PEERS:
+            other = lev_peer(lev, peer)
             pltpu.make_async_remote_copy(
                 src_ref=source.at[other],
                 dst_ref=target.at[lev],
@@ -237,14 +252,11 @@
                 device_id=(blk, other),
                 device_id_type=MESH,
             ).start()
-            return carry
-
-        lax.fori_loop(1, NL, step, 0)
         rows = pl.ds(0, NL - 1)
         return pltpu.make_async_remote_copy(
             src_ref=source.at[rows], dst_ref=target.at[rows],
             send_sem=send_sem.at[sem], recv_sem=recv_sem.at[sem],
-            device_id=(blk, (lev + 1) % NL), device_id_type=MESH,
+            device_id=(blk, lev_peer(lev, LEV_PEERS[0])), device_id_type=MESH,
         )
 
     sent_1 = send_blk(s1_ref, r1_ref, 0)
@@ -294,8 +306,9 @@
 
     sent_1.wait_recv()
 
+    rows_ref[...] = r1_ref[...].reshape(8 * NB, 128).astype(F32)
     for a in range(2):
-        block = stack([r1_ref[pl.ds(4 * a + j, NB, stride=8), :] for j in range(4)]).T.astype(BF16)
+        block = stack([rows_ref[pl.ds(4 * a + j, NB, stride=8), :] for j in range(4)]).T.astype(BF16)
         for t in range(8):
             s2_ref[2 * t + a] = block[16 * t : 16 * (t + 1)]
     r2_ref[lev] = s2_ref[lev]
@@ -309,9 +322,9 @@
     def chosen(q, e):
         return ((parity == q) & (side == e)).astype(F32).astype(BF16)
 
-    def solve_step(step, carry):
+    for step in range(2):
         for e in range(2):
-            columns = pl.ds(pl.multiple_of(256 * step, 256), 256)
+            columns = slice(256 * step, 256 * (step + 1))
             left = jnp.concatenate([data * chosen(0, e), data * chosen(1, e)], axis=1)
             spectral = dot(left, leg_ref[:, columns])
             high, low = split(spectral)
@@ -322,9 +335,6 @@
             both = dot(mode2_ref[...], high)
             change = both[:256] + both[256:] + dot(mode2_ref[:256], low)
             solved_ref[e, :, columns] = (spectral - change).astype(BF16)
-        return carry
-
-    lax.fori_loop(0, 2, solve_step, 0)
 
     picked = []
     for e in range(2):
@@ -338,14 +348,16 @@
     for a in range(2):
         block = stack([r3_ref[2 * t + a] for t in range(8)]).astype(F32).T
         for j in range(4):
-            s4_ref[pl.ds(4 * a + j, NB, stride=8), :] = block[NB * j : NB * (j + 1)]
-    r4_ref[own, :] = s4_ref[own, :]
+            rows_ref[pl.ds(4 * a + j, NB, stride=8), :] = block[NB * j : NB * (j + 1)]
+    s4_ref[...] = rows_ref[...].astype(BF16).reshape(NB, 8, 128)
+    r4_ref[blk] = s4_ref[blk]
     sent_4 = send_blk(s4_ref, r4_ref, 3)
     out_ref[:, :, :, pl.ds(LIVE, PSLOT - LIVE)] = jnp.zeros((2, 2, 4, PSLOT - LIVE), F32)
     sent_4.wait_recv()
 
+    rows_ref[...] = r4_ref[...].reshape(8 * NB, 128).astype(F32)
     for i in range(2):
-        four_ref[i] = stack([r4_ref[pl.ds(2 * a + i, NB, stride=8), :] for a in range(4)]).T
+        four_ref[i] = stack([rows_ref[pl.ds(2 * a + i, NB, stride=8), :] for a in range(4)]).T
 
     def turn_step(step, carry):
         i = step // TILES
@@ -364,17 +376,15 @@
                 imags.append(imag * c - real * s)
             for part, rows in enumerate((reals, imags)):
                 high, low = split(stack(rows))
-                lanes = slice(128 * part, 128 * (part + 1))
-                turned_ref[i, tile, 16 * k : 16 * k + 16, lanes] = high
-                turned_ref[i, tile, ROWS + 16 * k : ROWS + 16 * k + 16, lanes] = low
+                lanes = pl.ds(pl.multiple_of(256 * tile + 128 * part, 128), 128)
+                turned_ref[i, 16 * k : 16 * k + 16, lanes] = high
+                turned_ref[i, ROWS + 16 * k : ROWS + 16 * k + 16, lanes] = low
         return carry
 
     lax.fori_loop(0, 2 * TILES, turn_step, 0)
 
     for i in range(2):
-        left = jnp.concatenate([turned_ref[i, tile] for tile in range(TILES)], axis=1)
-        right = jnp.concatenate([table_ref[i, tile] for tile in range(TILES)], axis=1)
-        both = dot_nt(left, right)
+        both = dot_nt(turned_ref[i], table_ref[i])
         points = points_of(i)
         for u in range(BLOCKS):
             value = both[8 * u : 8 * u + 8] + both[ROWS + 8 * u : ROWS + 8 * u + 8]
@@ -392,7 +402,7 @@
     hbm = pl.BlockSpec(memory_space=pl.ANY)
     return pl.pallas_call(
         kernel,
-        out_shape=jax.ShapeDtypeStruct(grid_values.shape, F32),
+        out_shape=pltpu.VMEM(grid_values.shape, F32),
         in_specs=[hbm, smem, hbm, vmem, vmem, smem, vmem, smem],
         out_specs=vmem,
         scratch_shapes=[
@@ -400,29 +410,30 @@
             pltpu.VMEM((2, 2, 64, HALF), BF16),
             pltpu.VMEM((TILES, 8, 128), F32),
             pltpu.VMEM((2, 2, ROWS, SPAN), BF16),
-            pltpu.VMEM((2, TILES, SPAN, 256), BF16),
+            pltpu.VMEM((2, SPAN, 2 * WAVES), BF16),
             pltpu.VMEM((2, TILES, 2, BLOCKS, 8, 128), F32),
             pltpu.VMEM((2, 128, 128), F32),
             pltpu.VMEM((8 * NB, 128), F32),
-            pltpu.VMEM((8 * NB, 128), F32),
+            pltpu.VMEM((NB, 8, 128), BF16),
+            pltpu.VMEM((NB, 8, 128), BF16),
             pltpu.VMEM((NL, 16, 128), BF16),
             pltpu.VMEM((NL, 16, 128), BF16),
             pltpu.VMEM((NL, 16, 128), BF16),
             pltpu.VMEM((NL, 16, 128), BF16),
-            pltpu.VMEM((8 * NB, 128), F32),
-            pltpu.VMEM((8 * NB, 128), F32),
+            pltpu.VMEM((NB, 8, 128), BF16),
+            pltpu.VMEM((NB, 8, 128), BF16),
             pltpu.VMEM((256, HALF), BF16),
             pltpu.VMEM((512, 256), BF16),
             pltpu.VMEM((512, 256), BF16),
             pltpu.VMEM((2, 4, 256, 128), F32),
             pltpu.VMEM((2, 256, HALF), BF16),
-            pltpu.VMEM((2, TILES, 2 * ROWS, 256), BF16),
+            pltpu.VMEM((2, 2 * ROWS, 2 * WAVES), BF16),
             pltpu.SemaphoreType.DMA((2,)),
             pltpu.SemaphoreType.DMA((4,)),
             pltpu.SemaphoreType.DMA((4,)),
         ],
         compiler_params=pltpu.CompilerParams(
-            collective_id=0, has_side_effects=True, vmem_limit_bytes=62 * 1024 * 1024
+            collective_id=0, has_side_effects=True, vmem_limit_bytes=60 * 1024 * 1024
         ),
         cost_estimate=pl.CostEstimate(flops=4_000_000_000, bytes_accessed=1_500_000, transcendentals=0),
     )(

time: 48.9 us -> 43.2 us (0.88)
  Pallas kernels: 46.9 us -> 42.2 us
  local copies, waits for them, and re-layouts: 1.77 us -> 0.75 us
    pallas_call x1, Pallas kernels: 46.9 us -> 42.2 us  [shards(): pl.pallas_call(kernel, out_shape=pltpu.VMEM(grid_values.shape, F32), in_s...]
    unnamed x1, local copies, waits for them, and re-layouts: 1.77 us -> 0.75 us
where the time goes in v1:
time: 43.2 us; the launch traced here: 43 us
  Pallas kernels  42.2 us (98%)
  local copies, waits for them, and re-layouts  0.75 us (2%)
    pallas_call x1, Pallas kernels, shards(): pl.pallas_call(kernel, out_shape=pltpu.VMEM(grid_values.shape, F32), in_s...  42.2 us

profile of v1, /device:TPU:1, one launch (start us, length us, event | category | flops | bytes accessed | tf_op | source)
XLA Modules:
  0.0 43.0 jit_solution(8805101468217893482)
XLA Ops:
  0.0 42.2 %shard_map.73 = f32[2,2,4,6144]{3,2,1,0:T(4,128)S(1)} custom-call(f32[2,2,4,6144]{3,2,1,0:T(4,128)} %grid_hbm.1, f32[2]{0:T(128)} %weight_ref.1, bf16[32,2,64,512]{3,2,1,0:T(8,128)(2,1)} %legendre_hbm.1, f32[64,64]{1,0:T(8,128)} %modes_ref.1, f32[1,64]{1,0:T(1,128)} %bitcast.3, s32[2]{0:T(128)} %cycle_ref.1, s32[8,128]{1,0:T(8,128)} %bitcast.2, s32[1024]{0:T(1024)} %slot_smem.1), custom_call_target="tpu_custom_call" | custom-call | flops 4000000000 | bytes 1500000 | tf_op jit(solution)/shard_map/pallas_call | solution.py:403
  42.2 0.7 %copy.9 = f32[2,2,4,6144]{3,2,1,0:T(4,128)} copy(f32[2,2,4,6144]{3,2,1,0:T(4,128)S(1)} %shard_map.73) | data formatting | bytes 786432

commit v2 on v1

--- a/solution.py
+++ b/solution.py
@@ -98,9 +98,9 @@
 def kernel(
     grid_hbm, weight_ref, legendre_hbm, modes_ref, rates_ref, cycle_ref, slot_ref, slot_smem,
     out_ref,
-    grid_ref, raw_ref, wave_ref, x_ref, table_ref, turn_ref, four_ref,
+    grid_ref, raw_ref, wave_ref, x_ref, table_ref, rest_ref, turn_ref, four_ref,
     rows_ref, s1_ref, r1_ref, s2_ref, r2_ref, s3_ref, r3_ref, s4_ref, r4_ref,
-    leg_ref, mode1_ref, mode2_ref, damp_ref, solved_ref, turned_ref,
+    leg_ref, mode1_ref, mode2_ref, damp_ref, solved_ref,
     load_sem, send_sem, recv_sem,
 ):
     blk = lax.axis_index("blk")
@@ -133,6 +133,71 @@
 
     def points_of(i):
         return 20 + 4 * cycle_ref[i]
+
+    def rotations(i, tile):
+        points = jnp.full((8, 128), points_of(i), jnp.int32).astype(F32)
+        inverse = 1.0 / points
+        wave = wave_ref[tile]
+        row = iota((8, 128), 0)
+        place = row.astype(F32)
+        extra = jnp.where(row == 0, 8.0, jnp.where(row == 1, 128.0, 2048.0))
+        fine = rotation(place * wave, points, inverse)
+        coarse = rotation(16.0 * place * wave, points, inverse)
+        block = rotation(256.0 * place * wave, points, inverse)
+        jump = rotation(extra * wave, points, inverse)
+
+        def spread_row(pair, k):
+            return tuple(jnp.broadcast_to(part[k : k + 1], (8, 128)) for part in pair)
+
+        fine_next = turn(fine, spread_row(jump, 0))
+        coarse_next = turn(coarse, spread_row(jump, 1))
+        leap = spread_row(jump, 2)
+        kept = (2.0 * wave < points).astype(F32)
+        block = (block[0] * kept, block[1] * kept)
+        block_1 = turn(block, leap)
+        block_2 = turn(block_1, leap)
+
+        high = [[], []]
+        low = [[], []]
+        for a in range(16):
+            lead = spread_row(coarse if a < 8 else coarse_next, a % 8)
+            first = turn(lead, fine)
+            second = turn(lead, fine_next)
+            for part in range(2):
+                h, l = split(stack([first[part], second[part]]))
+                high[part].append(h)
+                low[part].append(l)
+        table = jnp.concatenate([stack(high[0]), stack(high[1])], axis=1)
+        rest = jnp.concatenate([stack(low[0]), stack(low[1])], axis=1)
+        table_ref[i, :, pl.ds(pl.multiple_of(256 * tile, 256), 256)] = table
+        turns = [spread_row((block, block_1, block_2)[u // 8], u % 8) for u in range(BLOCKS)]
+        for u in range(BLOCKS):
+            turn_ref[i, tile, 0, u], turn_ref[i, tile, 1, u] = turns[u]
+        return table, rest, turns
+
+    def transform(i, tile, table, rest, turns):
+        x_high = x_ref[i, 0]
+        sums = dot(
+            jnp.concatenate([x_high, x_ref[i, 1], x_high], axis=1),
+            jnp.concatenate([table, table, rest], axis=0),
+        )
+        real = jnp.zeros((8, 128), F32)
+        imag = jnp.zeros((8, 128), F32)
+        for u in range(BLOCKS):
+            c, s = turns[u]
+            p, q = sums[8 * u : 8 * u + 8, :128], sums[8 * u : 8 * u + 8, 128:]
+            real = real + (c * p - s * q)
+            imag = imag + (c * q + s * p)
+        start = pl.multiple_of(16 * tile, 16)
+        four_ref[i, pl.ds(start, 8), :] = real
+        four_ref[i, pl.ds(start + 8, 8), :] = imag
+
+    def early_step(tile, carry):
+        _, rest, _ = rotations(0, tile)
+        rest_ref[:, pl.ds(pl.multiple_of(256 * tile, 256), 256)] = rest
+        return carry
+
+    lax.fori_loop(0, 8, early_step, 0, unroll=8)
 
     grid_copy.wait()
 
@@ -154,66 +219,20 @@
         x_ref[i, 1, pl.ds(pl.multiple_of(16 * k, 16), 16), :] = low
         return carry
 
-    lax.fori_loop(0, BLOCKS, fold_step, 0)
+    lax.fori_loop(0, BLOCKS, fold_step, 0, unroll=2)
+
+    def early_transform(tile, carry):
+        lanes = pl.ds(pl.multiple_of(256 * tile, 256), 256)
+        turns = [(turn_ref[0, tile, 0, u], turn_ref[0, tile, 1, u]) for u in range(BLOCKS)]
+        transform(0, tile, table_ref[0, :, lanes], rest_ref[:, lanes], turns)
+        return carry
 
     def analyse_step(step, carry):
-        i = step // TILES
-        tile = step % TILES
-        points = jnp.full((8, 128), points_of(i), jnp.int32).astype(F32)
-        inverse = 1.0 / points
-        wave = wave_ref[tile]
-        row = iota((8, 128), 0)
-        place = row.astype(F32)
-        extra = jnp.where(row == 0, 8.0, jnp.where(row == 1, 128.0, 2048.0))
-        fine = rotation(place * wave, points, inverse)
-        coarse = rotation(16.0 * place * wave, points, inverse)
-        block = rotation(256.0 * place * wave, points, inverse)
-        jump = rotation(extra * wave, points, inverse)
-
-        def spread_row(pair, k, rows=8):
-            return tuple(jnp.broadcast_to(part[k : k + 1], (rows, 128)) for part in pair)
-
-        fine_next = turn(fine, spread_row(jump, 0))
-        coarse_next = turn(coarse, spread_row(jump, 1))
-        leap = spread_row(jump, 2)
-        kept = (2.0 * wave < points).astype(F32)
-        block = (block[0] * kept, block[1] * kept)
-        block_1 = turn(block, leap)
-        block_2 = turn(block_1, leap)
-
-        high = [[], []]
-        low = [[], []]
-        for a in range(16):
-            lead = spread_row(coarse if a < 8 else coarse_next, a % 8)
-            first = turn(lead, fine)
-            second = turn(lead, fine_next)
-            for part in range(2):
-                h, l = split(stack([first[part], second[part]]))
-                high[part].append(h)
-                low[part].append(l)
-        table = jnp.concatenate([stack(high[0]), stack(high[1])], axis=1)
-        rest = jnp.concatenate([stack(low[0]), stack(low[1])], axis=1)
-        table_ref[i, :, pl.ds(pl.multiple_of(256 * tile, 256), 256)] = table
-        x_high = x_ref[i, 0]
-        sums = dot(
-            jnp.concatenate([x_high, x_ref[i, 1], x_high], axis=1),
-            jnp.concatenate([table, table, rest], axis=0),
-        )
-        real = jnp.zeros((8, 128), F32)
-        imag = jnp.zeros((8, 128), F32)
-        for u in range(BLOCKS):
-            c, s = spread_row((block, block_1, block_2)[u // 8], u % 8)
-            turn_ref[i, tile, 0, u] = c
-            turn_ref[i, tile, 1, u] = s
-            p, q = sums[8 * u : 8 * u + 8, :128], sums[8 * u : 8 * u + 8, 128:]
-            real = real + (c * p - s * q)
-            imag = imag + (c * q + s * p)
-        start = pl.multiple_of(16 * tile, 16)
-        four_ref[i, pl.ds(start, 8), :] = real
-        four_ref[i, pl.ds(start + 8, 8), :] = imag
+        transform(step // TILES, step % TILES, *rotations(step // TILES, step % TILES))
         return carry
 
-    lax.fori_loop(0, 2 * TILES, analyse_step, 0, unroll=4)
+    lax.fori_loop(0, 8, early_transform, 0, unroll=8)
+    lax.fori_loop(8, 2 * TILES, analyse_step, 0, unroll=8)
 
     for i in range(2):
         flipped = four_ref[i].T
@@ -327,13 +346,11 @@
             columns = slice(256 * step, 256 * (step + 1))
             left = jnp.concatenate([data * chosen(0, e), data * chosen(1, e)], axis=1)
             spectral = dot(left, leg_ref[:, columns])
-            high, low = split(spectral)
-            both = dot(mode1_ref[...], high)
-            modal = both[:256] + both[256:] + dot(mode1_ref[:256], low)
+            both = dot(mode1_ref[...], spectral.astype(BF16))
+            modal = both[:256] + both[256:]
             damping = jnp.concatenate([damp_ref[e, 2 * step], damp_ref[e, 2 * step + 1]], axis=1)
-            high, low = split(modal * damping)
-            both = dot(mode2_ref[...], high)
-            change = both[:256] + both[256:] + dot(mode2_ref[:256], low)
+            both = dot(mode2_ref[...], (modal * damping).astype(BF16))
+            change = both[:256] + both[256:]
             solved_ref[e, :, columns] = (spectral - change).astype(BF16)
 
     picked = []
@@ -359,38 +376,30 @@
     for i in range(2):
         four_ref[i] = stack([rows_ref[pl.ds(2 * a + i, NB, stride=8), :] for a in range(4)]).T
 
-    def turn_step(step, carry):
-        i = step // TILES
-        tile = step % TILES
-        wave = wave_ref[tile]
-        double = jnp.where(wave == 0.0, 1.0, 2.0)
-        start = pl.multiple_of(16 * tile, 16)
-        real = four_ref[i, pl.ds(start, 8), :] * double
-        imag = four_ref[i, pl.ds(start + 8, 8), :] * double
-        for k in range(BLOCKS // 2):
-            reals, imags = [], []
-            for u in (2 * k, 2 * k + 1):
-                c = turn_ref[i, tile, 0, u]
-                s = turn_ref[i, tile, 1, u]
-                reals.append(real * c + imag * s)
-                imags.append(imag * c - real * s)
-            for part, rows in enumerate((reals, imags)):
-                high, low = split(stack(rows))
-                lanes = pl.ds(pl.multiple_of(256 * tile + 128 * part, 128), 128)
-                turned_ref[i, 16 * k : 16 * k + 16, lanes] = high
-                turned_ref[i, ROWS + 16 * k : ROWS + 16 * k + 16, lanes] = low
-        return carry
-
-    lax.fori_loop(0, 2 * TILES, turn_step, 0)
-
     for i in range(2):
-        both = dot_nt(turned_ref[i], table_ref[i])
         points = points_of(i)
+        value = 0.0
+        for group in range(2):
+            left = []
+            for tile in range(4 * group, 4 * group + 4):
+                double = jnp.where(wave_ref[tile] == 0.0, 1.0, 2.0)
+                real = four_ref[i, 16 * tile : 16 * tile + 8, :] * double
+                imag = four_ref[i, 16 * tile + 8 : 16 * tile + 16, :] * double
+                reals, imags = [], []
+                for u in range(BLOCKS):
+                    c = turn_ref[i, tile, 0, u]
+                    s = turn_ref[i, tile, 1, u]
+                    reals.append(real * c + imag * s)
+                    imags.append(imag * c - real * s)
+                left += [stack(reals).astype(BF16), stack(imags).astype(BF16)]
+            right = table_ref[i, :, 1024 * group : 1024 * (group + 1)]
+            value = value + dot_nt(jnp.concatenate(left, axis=1), right)
         for u in range(BLOCKS):
-            value = both[8 * u : 8 * u + 8] + both[ROWS + 8 * u : ROWS + 8 * u + 8]
+            even = value[8 * u : 8 * u + 4]
+            odd = value[8 * u + 4 : 8 * u + 8]
             live = iota((4, SPAN), 1) + SPAN * u < points
-            out_ref[i, 0, :, SPAN * u : SPAN * (u + 1)] = jnp.where(live, value[:4] + value[4:], 0.0)
-            out_ref[i, 1, :, SPAN * u : SPAN * (u + 1)] = jnp.where(live, value[:4] - value[4:], 0.0)
+            out_ref[i, 0, :, SPAN * u : SPAN * (u + 1)] = jnp.where(live, even + odd, 0.0)
+            out_ref[i, 1, :, SPAN * u : SPAN * (u + 1)] = jnp.where(live, even - odd, 0.0)
 
     for sent in (sent_1, sent_2, sent_3, sent_4):
         sent.wait_send()
@@ -411,6 +420,7 @@
             pltpu.VMEM((TILES, 8, 128), F32),
             pltpu.VMEM((2, 2, ROWS, SPAN), BF16),
             pltpu.VMEM((2, SPAN, 2 * WAVES), BF16),
+            pltpu.VMEM((SPAN, 2 * WAVES), BF16),
             pltpu.VMEM((2, TILES, 2, BLOCKS, 8, 128), F32),
             pltpu.VMEM((2, 128, 128), F32),
             pltpu.VMEM((8 * NB, 128), F32),
@@ -427,7 +437,6 @@
             pltpu.VMEM((512, 256), BF16),
             pltpu.VMEM((2, 4, 256, 128), F32),
             pltpu.VMEM((2, 256, HALF), BF16),
-            pltpu.VMEM((2, 2 * ROWS, 2 * WAVES), BF16),
             pltpu.SemaphoreType.DMA((2,)),
             pltpu.SemaphoreType.DMA((4,)),
             pltpu.SemaphoreType.DMA((4,)),

time: 43.2 us -> 41.5 us (0.961)
  Pallas kernels: 42.2 us -> 40.6 us
    pallas_call x1, Pallas kernels: 42.2 us -> 40.6 us  [shards(): pl.pallas_call(kernel, out_shape=pltpu.VMEM(grid_values.shape, F32), in_s...]
where the time goes in v2:
time: 41.5 us; the launch traced here: 41.3 us
  Pallas kernels  40.6 us (98%)
  local copies, waits for them, and re-layouts  0.75 us (2%)
    pallas_call x1, Pallas kernels, shards(): pl.pallas_call(kernel, out_shape=pltpu.VMEM(grid_values.shape, F32), in_s...  40.6 us

profile of v2, /device:TPU:1, one launch (start us, length us, event | category | flops | bytes accessed | tf_op | source)
XLA Modules:
  0.0 41.3 jit_solution(17116828098025205542)
XLA Ops:
  0.0 40.6 %shard_map.73 = f32[2,2,4,6144]{3,2,1,0:T(4,128)S(1)} custom-call(f32[2,2,4,6144]{3,2,1,0:T(4,128)} %grid_hbm.1, f32[2]{0:T(128)} %weight_ref.1, bf16[32,2,64,512]{3,2,1,0:T(8,128)(2,1)} %legendre_hbm.1, f32[64,64]{1,0:T(8,128)} %modes_ref.1, f32[1,64]{1,0:T(1,128)} %bitcast.3, s32[2]{0:T(128)} %cycle_ref.1, s32[8,128]{1,0:T(8,128)} %bitcast.2, s32[1024]{0:T(1024)} %slot_smem.1), custom_call_target="tpu_custom_call" | custom-call | flops 4000000000 | bytes 1500000 | tf_op jit(solution)/shard_map/pallas_call | solution.py:412
  40.6 0.7 %copy.9 = f32[2,2,4,6144]{3,2,1,0:T(4,128)} copy(f32[2,2,4,6144]{3,2,1,0:T(4,128)S(1)} %shard_map.73) | data formatting | bytes 786432

commit v3 on v2

--- a/solution.py
+++ b/solution.py
@@ -98,7 +98,7 @@
 def kernel(
     grid_hbm, weight_ref, legendre_hbm, modes_ref, rates_ref, cycle_ref, slot_ref, slot_smem,
     out_ref,
-    grid_ref, raw_ref, wave_ref, x_ref, table_ref, rest_ref, turn_ref, four_ref,
+    grid_ref, raw_ref, wave_ref, x_ref, table_ref, rest_ref, flip_ref, turn_ref, four_ref,
     rows_ref, s1_ref, r1_ref, s2_ref, r2_ref, s3_ref, r3_ref, s4_ref, r4_ref,
     leg_ref, mode1_ref, mode2_ref, damp_ref, solved_ref,
     load_sem, send_sem, recv_sem,
@@ -298,11 +298,11 @@
     tall = spread_rows((256, LEVELS), 0).astype(F32).astype(BF16)
     wide = spread_rows((LEVELS, 256), 1).astype(F32).astype(BF16)
     same = ((iota((256, 256), 0) >> 2) & 3) == ((iota((256, 256), 1) >> 2) & 3)
-    for part, modes in enumerate(split(modes_ref[...])):
-        full = dot(tall, dot(modes, wide).astype(BF16))
-        mode2_ref[256 * part : 256 * (part + 1), :] = jnp.where(same, full, 0.0).astype(BF16)
-        full = dot(tall, dot_tn(modes, wide).astype(BF16))
-        mode1_ref[256 * part : 256 * (part + 1), :] = jnp.where(same, full, 0.0).astype(BF16)
+    modes = modes_ref[...].astype(BF16)
+    full = dot(tall, dot(modes, wide).astype(BF16))
+    mode2_ref[...] = jnp.where(same, full, 0.0).astype(BF16)
+    full = dot(tall, dot_tn(modes, wide).astype(BF16))
+    mode1_ref[...] = jnp.where(same, full, 0.0).astype(BF16)
 
     rate = jnp.sum(
         jnp.where(spread_rows((256, LEVELS), 0), jnp.broadcast_to(rates_ref[...], (256, LEVELS)), 0.0),
@@ -323,6 +323,15 @@
 
     lax.fori_loop(0, 8, damp_step, 0)
 
+    def flip_step(step, carry):
+        i = step // TILES
+        tile = step % TILES
+        lanes = pl.ds(pl.multiple_of(256 * tile, 256), 256)
+        flip_ref[i, lanes, :] = table_ref[i, :, lanes].T
+        return carry
+
+    lax.fori_loop(0, 2 * TILES, flip_step, 0)
+
     sent_1.wait_recv()
 
     rows_ref[...] = r1_ref[...].reshape(8 * NB, 128).astype(F32)
@@ -341,17 +350,16 @@
     def chosen(q, e):
         return ((parity == q) & (side == e)).astype(F32).astype(BF16)
 
-    for step in range(2):
-        for e in range(2):
-            columns = slice(256 * step, 256 * (step + 1))
-            left = jnp.concatenate([data * chosen(0, e), data * chosen(1, e)], axis=1)
-            spectral = dot(left, leg_ref[:, columns])
-            both = dot(mode1_ref[...], spectral.astype(BF16))
-            modal = both[:256] + both[256:]
-            damping = jnp.concatenate([damp_ref[e, 2 * step], damp_ref[e, 2 * step + 1]], axis=1)
-            both = dot(mode2_ref[...], (modal * damping).astype(BF16))
-            change = both[:256] + both[256:]
-            solved_ref[e, :, columns] = (spectral - change).astype(BF16)
+    jobs = [(e, step) for step in range(2) for e in range(2)]
+    lefts = [jnp.concatenate([data * chosen(q, e) for q in range(2)], axis=1) for e in range(2)]
+    spectral = [dot(lefts[e], leg_ref[:, 256 * step : 256 * (step + 1)]) for e, step in jobs]
+    modal = [dot(mode1_ref[...], part.astype(BF16)) for part in spectral]
+    for k, (e, step) in enumerate(jobs):
+        damping = jnp.concatenate([damp_ref[e, 2 * step], damp_ref[e, 2 * step + 1]], axis=1)
+        modal[k] = (modal[k] * damping).astype(BF16)
+    for k, (e, step) in enumerate(jobs):
+        solved = spectral[k] - dot(mode2_ref[...], modal[k])
+        solved_ref[e, :, 256 * step : 256 * (step + 1)] = solved.astype(BF16)
 
     picked = []
     for e in range(2):
@@ -392,8 +400,8 @@
                     reals.append(real * c + imag * s)
                     imags.append(imag * c - real * s)
                 left += [stack(reals).astype(BF16), stack(imags).astype(BF16)]
-            right = table_ref[i, :, 1024 * group : 1024 * (group + 1)]
-            value = value + dot_nt(jnp.concatenate(left, axis=1), right)
+            right = flip_ref[i, 1024 * group : 1024 * (group + 1), :]
+            value = value + dot(jnp.concatenate(left, axis=1), right)
         for u in range(BLOCKS):
             even = value[8 * u : 8 * u + 4]
             odd = value[8 * u + 4 : 8 * u + 8]
@@ -421,6 +429,7 @@
             pltpu.VMEM((2, 2, ROWS, SPAN), BF16),
             pltpu.VMEM((2, SPAN, 2 * WAVES), BF16),
             pltpu.VMEM((SPAN, 2 * WAVES), BF16),
+            pltpu.VMEM((2, 2 * WAVES, SPAN), BF16),
             pltpu.VMEM((2, TILES, 2, BLOCKS, 8, 128), F32),
             pltpu.VMEM((2, 128, 128), F32),
             pltpu.VMEM((8 * NB, 128), F32),
@@ -433,8 +442,8 @@
             pltpu.VMEM((NB, 8, 128), BF16),
             pltpu.VMEM((NB, 8, 128), BF16),
             pltpu.VMEM((256, HALF), BF16),
-            pltpu.VMEM((512, 256), BF16),
-            pltpu.VMEM((512, 256), BF16),
+            pltpu.VMEM((256, 256), BF16),
+            pltpu.VMEM((256, 256), BF16),
             pltpu.VMEM((2, 4, 256, 128), F32),
             pltpu.VMEM((2, 256, HALF), BF16),
             pltpu.SemaphoreType.DMA((2,)),

time: 41.5 us -> 40 us (0.964)
  Pallas kernels: 40.6 us -> 39.1 us
    pallas_call x1, Pallas kernels: 40.6 us -> 39.1 us  [shards(): pl.pallas_call(kernel, out_shape=pltpu.VMEM(grid_values.shape, F32), in_s...]
where the time goes in v3:
time: 40 us; the launch traced here: 39.8 us
  Pallas kernels  39.1 us (98%)
  local copies, waits for them, and re-layouts  0.75 us (2%)
    pallas_call x1, Pallas kernels, shards(): pl.pallas_call(kernel, out_shape=pltpu.VMEM(grid_values.shape, F32), in_s...  39.1 us

profile of v3, /device:TPU:1, one launch (start us, length us, event | category | flops | bytes accessed | tf_op | source)
XLA Modules:
  0.0 39.8 jit_solution(13506140518647615965)
XLA Ops:
  0.0 39.1 %shard_map.73 = f32[2,2,4,6144]{3,2,1,0:T(4,128)S(1)} custom-call(f32[2,2,4,6144]{3,2,1,0:T(4,128)} %grid_hbm.1, f32[2]{0:T(128)} %weight_ref.1, bf16[32,2,64,512]{3,2,1,0:T(8,128)(2,1)} %legendre_hbm.1, f32[64,64]{1,0:T(8,128)} %modes_ref.1, f32[1,64]{1,0:T(1,128)} %bitcast.3, s32[2]{0:T(128)} %cycle_ref.1, s32[8,128]{1,0:T(8,128)} %bitcast.2, s32[1024]{0:T(1024)} %slot_smem.1), custom_call_target="tpu_custom_call" | custom-call | flops 4000000000 | bytes 1500000 | tf_op jit(solution)/shard_map/pallas_call | solution.py:420
  39.1 0.7 %copy.9 = f32[2,2,4,6144]{3,2,1,0:T(4,128)} copy(f32[2,2,4,6144]{3,2,1,0:T(4,128)S(1)} %shard_map.73) | data formatting | bytes 786432

commit v4 on v3

--- a/solution.py
+++ b/solution.py
@@ -96,9 +96,9 @@
 
 
 def kernel(
-    grid_hbm, weight_ref, legendre_hbm, modes_ref, rates_ref, cycle_ref, slot_ref, slot_smem,
+    grid_hbm, weight_hbm, legendre_hbm, modes_hbm, rates_hbm, cycle_hbm, slot_hbm, slots_hbm,
     out_ref,
-    grid_ref, raw_ref, wave_ref, x_ref, table_ref, rest_ref, flip_ref, turn_ref, four_ref,
+    weight_ref, cycle_ref, slot_smem, slot_ref, modes_ref, rates_ref, grid_ref, raw_ref, wave_ref, x_ref, table_ref, rest_ref, flip_ref, turn_ref, four_ref,
     rows_ref, s1_ref, r1_ref, s2_ref, r2_ref, s3_ref, r3_ref, s4_ref, r4_ref,
     leg_ref, mode1_ref, mode2_ref, damp_ref, solved_ref,
     load_sem, send_sem, recv_sem,
@@ -107,20 +107,28 @@
     lev = lax.axis_index("lev")
 
     barrier = pltpu.get_barrier_semaphore()
-
+    for peer in BLK_PEERS:
+        pl.semaphore_signal(barrier, inc=1, device_id=(blk_peer(blk, peer), lev), device_id_type=MESH)
+    for peer in LEV_PEERS:
+        pl.semaphore_signal(barrier, inc=1, device_id=(blk, lev_peer(lev, peer)), device_id_type=MESH)
+
+    small = [
+        (slot_hbm, slot_ref), (cycle_hbm, cycle_ref), (weight_hbm, weight_ref),
+        (slots_hbm, slot_smem), (modes_hbm, modes_ref), (rates_hbm, rates_ref),
+    ]
+    small_copies = [pltpu.make_async_copy(a, b, load_sem.at[2 + k]) for k, (a, b) in enumerate(small)]
+    for copy in small_copies:
+        copy.start()
     grid_copy = pltpu.make_async_copy(grid_hbm, grid_ref, load_sem.at[0])
     grid_copy.start()
     legendre_copy = pltpu.make_async_copy(
         legendre_hbm.at[pl.ds(2 * lev, 2)], raw_ref, load_sem.at[1]
     )
     legendre_copy.start()
-    for peer in BLK_PEERS:
-        pl.semaphore_signal(barrier, inc=1, device_id=(blk_peer(blk, peer), lev), device_id_type=MESH)
-    for peer in LEV_PEERS:
-        pl.semaphore_signal(barrier, inc=1, device_id=(blk, lev_peer(lev, peer)), device_id_type=MESH)
-
     column = iota((128, WAVES), 1)
     pick = (iota((128, WAVES), 0) == 32 * (column & 3) + (column >> 5)).astype(F32).astype(BF16)
+    for copy in small_copies[:3]:
+        copy.wait()
     slots = slot_ref[...]
     halves = stack([slots >> 5, slots & 31]).astype(F32).astype(BF16)
     spread = dot(halves, pick)
@@ -281,6 +289,8 @@
     sent_1 = send_blk(s1_ref, r1_ref, 0)
 
     legendre_copy.wait()
+    for copy in small_copies[3:]:
+        copy.wait()
     wave_0 = slot_smem[32 * blk + 2 * lev]
     wave_1 = slot_smem[32 * blk + 2 * lev + 1]
     row = iota((256, 256), 0)
@@ -298,11 +308,11 @@
     tall = spread_rows((256, LEVELS), 0).astype(F32).astype(BF16)
     wide = spread_rows((LEVELS, 256), 1).astype(F32).astype(BF16)
     same = ((iota((256, 256), 0) >> 2) & 3) == ((iota((256, 256), 1) >> 2) & 3)
-    modes = modes_ref[...].astype(BF16)
-    full = dot(tall, dot(modes, wide).astype(BF16))
-    mode2_ref[...] = jnp.where(same, full, 0.0).astype(BF16)
-    full = dot(tall, dot_tn(modes, wide).astype(BF16))
-    mode1_ref[...] = jnp.where(same, full, 0.0).astype(BF16)
+    for part, modes in enumerate(split(modes_ref[...])):
+        full = dot(tall, dot(modes, wide).astype(BF16))
+        mode2_ref[256 * part : 256 * (part + 1), :] = jnp.where(same, full, 0.0).astype(BF16)
+        full = dot(tall, dot_tn(modes, wide).astype(BF16))
+        mode1_ref[256 * part : 256 * (part + 1), :] = jnp.where(same, full, 0.0).astype(BF16)
 
     rate = jnp.sum(
         jnp.where(spread_rows((256, LEVELS), 0), jnp.broadcast_to(rates_ref[...], (256, LEVELS)), 0.0),
@@ -354,11 +364,13 @@
     lefts = [jnp.concatenate([data * chosen(q, e) for q in range(2)], axis=1) for e in range(2)]
     spectral = [dot(lefts[e], leg_ref[:, 256 * step : 256 * (step + 1)]) for e, step in jobs]
     modal = [dot(mode1_ref[...], part.astype(BF16)) for part in spectral]
+    modal = [part[:256] + part[256:] for part in modal]
     for k, (e, step) in enumerate(jobs):
         damping = jnp.concatenate([damp_ref[e, 2 * step], damp_ref[e, 2 * step + 1]], axis=1)
         modal[k] = (modal[k] * damping).astype(BF16)
     for k, (e, step) in enumerate(jobs):
-        solved = spectral[k] - dot(mode2_ref[...], modal[k])
+        change = dot(mode2_ref[...], modal[k])
+        solved = spectral[k] - (change[:256] + change[256:])
         solved_ref[e, :, 256 * step : 256 * (step + 1)] = solved.astype(BF16)
 
     picked = []
@@ -415,14 +427,19 @@
 
 def shards(grid_values, quad_weight, legendre, vertical_modes, eigenvalues, pair_latitude, wave_slot):
     vmem = pl.BlockSpec(memory_space=pltpu.VMEM)
-    smem = pl.BlockSpec(memory_space=pltpu.SMEM)
     hbm = pl.BlockSpec(memory_space=pl.ANY)
     return pl.pallas_call(
         kernel,
         out_shape=pltpu.VMEM(grid_values.shape, F32),
-        in_specs=[hbm, smem, hbm, vmem, vmem, smem, vmem, smem],
+        in_specs=[hbm] * 8,
         out_specs=vmem,
         scratch_shapes=[
+            pltpu.SMEM((2,), F32),
+            pltpu.SMEM((2,), jnp.int32),
+            pltpu.SMEM((WAVES,), jnp.int32),
+            pltpu.VMEM((8, 128), jnp.int32),
+            pltpu.VMEM((LEVELS, LEVELS), F32),
+            pltpu.VMEM((1, LEVELS), F32),
             pltpu.VMEM((2, 2, 4, PSLOT), F32),
             pltpu.VMEM((2, 2, 64, HALF), BF16),
             pltpu.VMEM((TILES, 8, 128), F32),
@@ -442,11 +459,11 @@
             pltpu.VMEM((NB, 8, 128), BF16),
             pltpu.VMEM((NB, 8, 128), BF16),
             pltpu.VMEM((256, HALF), BF16),
-            pltpu.VMEM((256, 256), BF16),
-            pltpu.VMEM((256, 256), BF16),
+            pltpu.VMEM((512, 256), BF16),
+            pltpu.VMEM((512, 256), BF16),
             pltpu.VMEM((2, 4, 256, 128), F32),
             pltpu.VMEM((2, 256, HALF), BF16),
-            pltpu.SemaphoreType.DMA((2,)),
+            pltpu.SemaphoreType.DMA((8,)),
             pltpu.SemaphoreType.DMA((4,)),
             pltpu.SemaphoreType.DMA((4,)),
         ],

time: 40 us -> 39.3 us (0.982)
  Pallas kernels: 39.1 us -> 38.4 us
    pallas_call x1, Pallas kernels: 39.1 us -> 38.4 us  [shards(): pl.pallas_call(kernel, out_shape=pltpu.VMEM(grid_values.shape, F32), in_s...]
where the time goes in v4:
time: 39.3 us; the launch traced here: 39.2 us
  Pallas kernels  38.4 us (98%)
  local copies, waits for them, and re-layouts  0.75 us (2%)
    pallas_call x1, Pallas kernels, shards(): pl.pallas_call(kernel, out_shape=pltpu.VMEM(grid_values.shape, F32), in_s...  38.4 us

profile of v4, /device:TPU:1, one launch (start us, length us, event | category | flops | bytes accessed | tf_op | source)
XLA Modules:
  0.0 39.2 jit_solution(15617500448068749940)
XLA Ops:
  0.0 38.4 %shard_map.73 = f32[2,2,4,6144]{3,2,1,0:T(4,128)S(1)} custom-call(f32[2,2,4,6144]{3,2,1,0:T(4,128)} %grid_hbm.1, f32[2]{0:T(128)} %weight_hbm.1, bf16[32,2,64,512]{3,2,1,0:T(8,128)(2,1)} %legendre_hbm.1, f32[64,64]{1,0:T(8,128)} %modes_hbm.1, f32[1,64]{1,0:T(1,128)} %bitcast.3, s32[2]{0:T(128)} %cycle_hbm.1, s32[8,128]{1,0:T(8,128)} %bitcast.2, s32[1024]{0:T(1024)} %slots_hbm.1), custom_call_target="tpu_custom_call" | custom-call | flops 4000000000 | bytes 1500000 | tf_op jit(solution)/shard_map/pallas_call | solution.py:431
  38.4 0.7 %copy.9 = f32[2,2,4,6144]{3,2,1,0:T(4,128)} copy(f32[2,2,4,6144]{3,2,1,0:T(4,128)S(1)} %shard_map.73) | data formatting | bytes 786432

commit v5 on v4

--- a/solution.py
+++ b/solution.py
@@ -107,11 +107,11 @@
     lev = lax.axis_index("lev")
 
     barrier = pltpu.get_barrier_semaphore()
-    for peer in BLK_PEERS:
-        pl.semaphore_signal(barrier, inc=1, device_id=(blk_peer(blk, peer), lev), device_id_type=MESH)
-    for peer in LEV_PEERS:
-        pl.semaphore_signal(barrier, inc=1, device_id=(blk, lev_peer(lev, peer)), device_id_type=MESH)
-
+    greetings = [(ring(y, 8) + ring(x, 4), "blk", (y, x)) for y, x in BLK_PEERS]
+    greetings += [(ring(z, 8) + 0.75 * c, "lev", (z, c)) for z, c in LEV_PEERS]
+    for _, axis, peer in sorted(greetings, reverse=True):
+        target = (blk_peer(blk, peer), lev) if axis == "blk" else (blk, lev_peer(lev, peer))
+        pl.semaphore_signal(barrier, inc=1, device_id=target, device_id_type=MESH)
     small = [
         (slot_hbm, slot_ref), (cycle_hbm, cycle_ref), (weight_hbm, weight_ref),
         (slots_hbm, slot_smem), (modes_hbm, modes_ref), (rates_hbm, rates_ref),
@@ -268,9 +268,8 @@
             device_id=(blk_peer(blk, BLK_PEERS[0]), lev), device_id_type=MESH,
         )
 
-    def send_lev(source, target, sem):
-        for peer in LEV_PEERS:
-            other = lev_peer(lev, peer)
+    def send_lev(source, target, sem, core=None):
+        def start(other):
             pltpu.make_async_remote_copy(
                 src_ref=source.at[other],
                 dst_ref=target.at[lev],
@@ -279,6 +278,14 @@
                 device_id=(blk, other),
                 device_id_type=MESH,
             ).start()
+
+        if core is None:
+            for peer in LEV_PEERS:
+                start(lev_peer(lev, peer))
+        else:
+            for step in sorted(range(1, 8), key=lambda z: -ring(z, 8)):
+                start((lev // 2 + step) % 8 * 2 + core)
+            pl.when(lev % 2 != core)(lambda: start(lev // 2 * 2 + core))
         rows = pl.ds(0, NL - 1)
         return pltpu.make_async_remote_copy(
             src_ref=source.at[rows], dst_ref=target.at[rows],
@@ -349,17 +356,17 @@
         block = stack([rows_ref[pl.ds(4 * a + j, NB, stride=8), :] for j in range(4)]).T.astype(BF16)
         for t in range(8):
             s2_ref[2 * t + a] = block[16 * t : 16 * (t + 1)]
+        sent_2 = send_lev(s2_ref, r2_ref, 1, a)
     r2_ref[lev] = s2_ref[lev]
-    sent_2 = send_lev(s2_ref, r2_ref, 1)
-    sent_2.wait_recv()
-
-    data = r2_ref[...].reshape(256, 128)
     parity = (iota((256, 128), 0) >> 2) & 1
     side = iota((256, 128), 1) >> 6
 
     def chosen(q, e):
         return ((parity == q) & (side == e)).astype(F32).astype(BF16)
 
+    sent_2.wait_recv()
+
+    data = r2_ref[...].reshape(256, 128)
     jobs = [(e, step) for step in range(2) for e in range(2)]
     lefts = [jnp.concatenate([data * chosen(q, e) for q in range(2)], axis=1) for e in range(2)]
     spectral = [dot(lefts[e], leg_ref[:, 256 * step : 256 * (step + 1)]) for e, step in jobs]
@@ -378,8 +385,8 @@
         back = dot_nt(solved_ref[e], leg_ref[...])
         picked.append(jnp.where(parity == 0, back[:, :128], back[:, 128:]))
     s3_ref[...] = jnp.where(side == 0, picked[0], picked[1]).astype(BF16).reshape(NL, 16, 128)
+    sent_3 = send_lev(s3_ref, r3_ref, 2)
     r3_ref[lev] = s3_ref[lev]
-    sent_3 = send_lev(s3_ref, r3_ref, 2)
     sent_3.wait_recv()
 
     for a in range(2):
@@ -387,8 +394,8 @@
         for j in range(4):
             rows_ref[pl.ds(4 * a + j, NB, stride=8), :] = block[NB * j : NB * (j + 1)]
     s4_ref[...] = rows_ref[...].astype(BF16).reshape(NB, 8, 128)
+    sent_4 = send_blk(s4_ref, r4_ref, 3)
     r4_ref[blk] = s4_ref[blk]
-    sent_4 = send_blk(s4_ref, r4_ref, 3)
     out_ref[:, :, :, pl.ds(LIVE, PSLOT - LIVE)] = jnp.zeros((2, 2, 4, PSLOT - LIVE), F32)
     sent_4.wait_recv()
 

time: 39.3 us -> 39.2 us (level)
  no operation moved by 1% of the time
where the time goes in v5:
time: 39.2 us; the launch traced here: 39.1 us
  Pallas kernels  38.3 us (98%)
  local copies, waits for them, and re-layouts  0.75 us (2%)
    pallas_call x1, Pallas kernels, shards(): pl.pallas_call(kernel, out_shape=pltpu.VMEM(grid_values.shape, F32), in_s...  38.3 us

profile of v5, /device:TPU:1, one launch (start us, length us, event | category | flops | bytes accessed | tf_op | source)
XLA Modules:
  0.0 39.1 jit_solution(4655961178224896072)
XLA Ops:
  0.0 38.3 %shard_map.73 = f32[2,2,4,6144]{3,2,1,0:T(4,128)S(1)} custom-call(f32[2,2,4,6144]{3,2,1,0:T(4,128)} %grid_hbm.1, f32[2]{0:T(128)} %weight_hbm.1, bf16[32,2,64,512]{3,2,1,0:T(8,128)(2,1)} %legendre_hbm.1, f32[64,64]{1,0:T(8,128)} %modes_hbm.1, f32[1,64]{1,0:T(1,128)} %bitcast.3, s32[2]{0:T(128)} %cycle_hbm.1, s32[8,128]{1,0:T(8,128)} %bitcast.2, s32[1024]{0:T(1024)} %slots_hbm.1), custom_call_target="tpu_custom_call" | custom-call | flops 4000000000 | bytes 1500000 | tf_op jit(solution)/shard_map/pallas_call | solution.py:438
  38.3 0.7 %copy.9 = f32[2,2,4,6144]{3,2,1,0:T(4,128)} copy(f32[2,2,4,6144]{3,2,1,0:T(4,128)S(1)} %shard_map.73) | data formatting | bytes 786432

commit v6 on v4

--- a/solution.py
+++ b/solution.py
@@ -205,7 +205,7 @@
         rest_ref[:, pl.ds(pl.multiple_of(256 * tile, 256), 256)] = rest
         return carry
 
-    lax.fori_loop(0, 8, early_step, 0, unroll=8)
+    lax.fori_loop(0, 8, early_step, 0, unroll=4)
 
     grid_copy.wait()
 
@@ -239,8 +239,8 @@
         transform(step // TILES, step % TILES, *rotations(step // TILES, step % TILES))
         return carry
 
-    lax.fori_loop(0, 8, early_transform, 0, unroll=8)
-    lax.fori_loop(8, 2 * TILES, analyse_step, 0, unroll=8)
+    lax.fori_loop(0, 8, early_transform, 0, unroll=4)
+    lax.fori_loop(8, 2 * TILES, analyse_step, 0, unroll=4)
 
     for i in range(2):
         flipped = four_ref[i].T

time: 39.3 us -> 39.3 us (level)
  no operation moved by 1% of the time
where the time goes in v6:
time: 39.3 us; the launch traced here: 39.2 us
  Pallas kernels  38.4 us (98%)
  local copies, waits for them, and re-layouts  0.75 us (2%)
    pallas_call x1, Pallas kernels, shards(): pl.pallas_call(kernel, out_shape=pltpu.VMEM(grid_values.shape, F32), in_s...  38.4 us

profile of v6, /device:TPU:1, one launch (start us, length us, event | category | flops | bytes accessed | tf_op | source)
XLA Modules:
  0.0 39.2 jit_solution(10911123694003834279)
XLA Ops:
  0.0 38.4 %shard_map.73 = f32[2,2,4,6144]{3,2,1,0:T(4,128)S(1)} custom-call(f32[2,2,4,6144]{3,2,1,0:T(4,128)} %grid_hbm.1, f32[2]{0:T(128)} %weight_hbm.1, bf16[32,2,64,512]{3,2,1,0:T(8,128)(2,1)} %legendre_hbm.1, f32[64,64]{1,0:T(8,128)} %modes_hbm.1, f32[1,64]{1,0:T(1,128)} %bitcast.3, s32[2]{0:T(128)} %cycle_hbm.1, s32[8,128]{1,0:T(8,128)} %bitcast.2, s32[1024]{0:T(1024)} %slots_hbm.1), custom_call_target="tpu_custom_call" | custom-call | flops 4000000000 | bytes 1500000 | tf_op jit(solution)/shard_map/pallas_call | solution.py:431
  38.4 0.7 %copy.9 = f32[2,2,4,6144]{3,2,1,0:T(4,128)} copy(f32[2,2,4,6144]{3,2,1,0:T(4,128)S(1)} %shard_map.73) | data formatting | bytes 786432
